TPU v7x, 32 devices: a whole 2x2x4 slice. The times are simulated.
32 devices in a mesh: dp: 8 (over z, y), row: 2 (over core), col: 2 (over x).
Axes of the slice: x: 2, y: 2, z: 4, core: 2. Of those that a mesh axis runs over, the one named last changes fastest.
Arguments:
- block_input: bfloat16 [4096, 2560], P(('dp', 'col')), may hold values from -6 to 6
- cotangent: bfloat16 [4096, 2560], P(('dp', 'col'), 'row'), may hold values from -6 to 6
- seq_lengths: int32 [32], replicated, may hold values from 16 to 128, as said below
- seq_owner: int32 [32], replicated, may hold values from 0 to 15, as said below
- norm_gain: bfloat16 [2560], P('row'), may hold values from 0.5 to 1.5
- proj_zx: bfloat16 [2560, 2, 5120], P('row', None, 'col'), may hold values from -0.125 to 0.125
- proj_bc: bfloat16 [2560, 256], P('row'), may hold values from -0.125 to 0.125
- proj_dt: bfloat16 [2560, 80], P('row', 'col'), may hold values from -0.125 to 0.125
- proj_out: bfloat16 [5120, 2560], P('col', 'row'), may hold values from -0.078125 to 0.078125
- inner_kernel: float32 [4, 5120], P(None, 'col'), may hold values from -3 to 3
- inner_offset: float32 [5120], P('col'), may hold values from -1.5 to 1.5
- shared_kernel: float32 [4, 256], replicated, may hold values from -3 to 3
- shared_offset: float32 [256], replicated, may hold values from -1.5 to 1.5
- decay_log: float32 [80], P('col'), may hold values from 0 to 2.77
- step_bias: float32 [80], P('col'), may hold values from -6 to -2
- skip_gain: float32 [80], P('col'), may hold values from 0.5 to 1.5
- output_gain: bfloat16 [5120], P('col'), may hold values from 0.5 to 1.5
Outputs:
- block_output: bfloat16 [4096, 2560], P(('dp', 'col'), 'row')
- input_grad: float32 [4096, 2560], P(('dp', 'col'), 'row')
- grad_norm: float32 [2560], P('row')
- grad_inproj: float32 [2560, 2, 5120], P('row', None, 'col')
- grad_shared: float32 [2560, 256], P('row')
- grad_steps: float32 [2560, 80], P('row', 'col')
- grad_outproj: float32 [5120, 2560], P('col', 'row')
- grad_kernel: float32 [4, 5120], P(None, 'col')
- grad_offset: float32 [5120], P('col')
- grad_skernel: float32 [4, 256], replicated
- grad_soffset: float32 [256], replicated
- grad_decay: float32 [80], P('col')
- grad_stepbias: float32 [80], P('col')
- grad_skip: float32 [80], P('col')
- grad_ogain: float32 [5120], P('col')
Inputs may be any that keep to these rules, and one draw needn't show every extreme that they name: `seq_lengths`: the lengths of the 2 sequences of one bucket sum to at most 256; in every draw some bucket holds 2 sequences of exactly 128 rows, so that its sum is 256. `seq_owner`: every bucket owns exactly 2 sequences.
All inputs are finite; a program needn't handle non-finite values.
Results may differ from a plain program's by a relative error of at most 0.0079.
The roundings to bfloat16 on the way count: a program that leaves them out, or rounds other values in their place, can miss the bound.
Values may be sent and summed in bfloat16 or wider, within the bound.
A program may use at most 256 MiB of HBM per device.

v0:
```python
import jax
import jax.numpy as jnp
from jax import lax
from jax.sharding import PartitionSpec as P

D = 2560
DI = 5120
SCAN_BLOCK = 256
CAP = 256
EPSILON = 1e-05
PRECISE = lax.Precision.HIGHEST


def layout(seq_lengths, seq_owner, bucket, capacity):
    owned = seq_owner == bucket
    owned_len = jnp.where(owned, seq_lengths, 0)
    starts = jnp.cumsum(owned_len) - owned_len
    places = jnp.arange(capacity, dtype=jnp.int32)[:, None]
    ends = starts + seq_lengths
    inside = owned[None, :] & (places >= starts[None, :]) & (places < ends[None, :])
    live_rows = jnp.any(inside, axis=1)
    seq_index = jnp.arange(seq_lengths.shape[0], dtype=jnp.int32)
    seq_ids = jnp.sum(jnp.where(inside, seq_index[None, :], 0), axis=1)
    seq_ids = jnp.where(live_rows, seq_ids, -1)
    return (seq_ids, live_rows.astype(jnp.float32))


def convolve(channels, kernel, offset, seq_ids, live_rows):
    tap_count = kernel.shape[0]
    summed_in = offset[None, :] + kernel[tap_count - 1][None, :] * channels
    for lag_steps in range(1, tap_count):
        lagged = jnp.concatenate(
            [jnp.zeros((lag_steps, channels.shape[1]), jnp.float32), channels[:-lag_steps]], axis=0
        )
        prior_ids = jnp.concatenate([jnp.full((lag_steps,), -1, jnp.int32), seq_ids[:-lag_steps]])
        same_seq = jnp.where((prior_ids == seq_ids) & (live_rows > 0), 1.0, 0.0).astype(jnp.float32)
        summed_in = (
            summed_in + kernel[tap_count - 1 - lag_steps][None, :] * lagged * same_seq[:, None]
        )
    return summed_in


def scan_blocks(
    values, inputs_b, inputs_c, step_sizes, decay_rate, skip_gain, seq_ids, live_rows, block_len
):
    rows_all, head_count, head_dim = values.shape
    state_size = inputs_b.shape[1]
    block_count = rows_all // block_len
    lower = jnp.arange(block_len)[:, None] >= jnp.arange(block_len)[None, :]

    def one_block(carried_in, block_item):
        memory, last_id = carried_in
        vals, bmat, cmat, sizes, rates, ids_here, live_here = block_item
        cumulated = jnp.cumsum(rates, axis=0)
        pair_live = (
            (ids_here[:, None] == ids_here[None, :])
            & (live_here[:, None] > 0)
            & (live_here[None, :] > 0)
            & lower
        )
        pair_mask = pair_live.astype(jnp.float32)
        scores = jnp.dot(cmat, bmat.T, precision=PRECISE)
        gap = jnp.where(pair_live[:, :, None], cumulated[:, None, :] - cumulated[None, :, :], 0.0)
        weights = jnp.exp(gap) * (pair_mask * scores)[:, :, None] * sizes[None, :, :]
        within = jnp.einsum("tsh,shp->thp", weights, vals, precision=PRECISE)
        carried = jnp.where((ids_here == last_id) & (live_here > 0), 1.0, 0.0).astype(jnp.float32)
        recalled = jnp.einsum("hpn,tn->thp", memory, cmat, precision=PRECISE)
        recalled = recalled * (jnp.exp(cumulated) * carried[:, None])[:, :, None]
        mixed_out = (within + recalled + skip_gain[None, :, None] * vals) * live_here[:, None, None]
        factor = jnp.exp(cumulated[-1][None, :] - cumulated) * pair_mask[-1][:, None] * sizes
        fresh_state = jnp.einsum("sh,shp,sn->hpn", factor, vals, bmat, precision=PRECISE)
        continues = jnp.where((ids_here[-1] == last_id) & (live_here[-1] > 0), 1.0, 0.0).astype(
            jnp.float32
        )
        memory = continues * jnp.exp(cumulated[-1])[:, None, None] * memory + fresh_state
        return ((memory, ids_here[-1]), mixed_out)

    items = (
        values.reshape(block_count, block_len, head_count, head_dim),
        inputs_b.reshape(block_count, block_len, state_size),
        inputs_c.reshape(block_count, block_len, state_size),
        step_sizes.reshape(block_count, block_len, head_count),
        decay_rate.reshape(block_count, block_len, head_count),
        seq_ids.reshape(block_count, block_len),
        live_rows.reshape(block_count, block_len),
    )
    start_state = (jnp.zeros((head_count, head_dim, state_size), jnp.float32), jnp.int32(-2))
    _, outputs = lax.scan(jax.checkpoint(one_block), start_state, items)
    return outputs.reshape(rows_all, head_count * head_dim)


def mixer_local(
    mixer_in,
    inner_kernel,
    inner_offset,
    shared_kernel,
    shared_offset,
    decay_log,
    step_bias,
    skip_gain,
    seq_ids,
    live_rows,
    block_len,
):
    inner_size = inner_kernel.shape[1]
    state_size = shared_kernel.shape[1] // 2
    head_count = decay_log.shape[0]
    gate_in = mixer_in[:, :inner_size]
    conv_in = mixer_in[:, inner_size : 2 * inner_size]
    shared_in = mixer_in[:, 2 * inner_size : 2 * inner_size + 2 * state_size]
    step_raw = mixer_in[:, 2 * inner_size + 2 * state_size :]
    mixed_x = jax.nn.silu(convolve(conv_in, inner_kernel, inner_offset, seq_ids, live_rows))
    mixed_bc = jax.nn.silu(convolve(shared_in, shared_kernel, shared_offset, seq_ids, live_rows))
    step_sizes = jax.nn.softplus(step_raw + step_bias[None, :])
    decay_rate = step_sizes * (-jnp.exp(decay_log))[None, :]
    values = mixed_x.reshape(mixed_x.shape[0], head_count, inner_size // head_count)
    ssm_out = scan_blocks(
        values,
        mixed_bc[:, :state_size],
        mixed_bc[:, state_size:],
        step_sizes,
        decay_rate,
        skip_gain,
        seq_ids,
        live_rows,
        block_len,
    )
    return ssm_out * jax.nn.silu(gate_in)


def per_device(
    block_input,
    cotangent,
    seq_lengths,
    seq_owner,
    norm_gain,
    proj_zx,
    proj_bc,
    proj_dt,
    proj_out,
    inner_kernel,
    inner_offset,
    shared_kernel,
    shared_offset,
    decay_log,
    step_bias,
    skip_gain,
    output_gain,
):
    row_count = lax.axis_size("row")
    col_count = lax.axis_size("col")
    row_index = lax.axis_index("row")
    col_index = lax.axis_index("col")
    data_index = lax.axis_index("dp")
    width_part = norm_gain.shape[0]
    inner_size = proj_zx.shape[2]
    state_size = proj_bc.shape[1] // 2
    tap_count = inner_kernel.shape[0]
    capacity = CAP
    bucket = data_index * row_count + row_index
    seq_ids, live_rows = layout(seq_lengths, seq_owner, bucket, capacity)
    rscale = lax.rsqrt(
        jnp.mean(jnp.square(block_input.astype(jnp.float32)), axis=1, keepdims=True) + EPSILON
    )
    own_cols = lax.dynamic_slice_in_dim(block_input, row_index * width_part, width_part, 1).astype(
        jnp.float32
    )
    normalized = own_cols * rscale
    gain_f = norm_gain.astype(jnp.float32)
    normed = (normalized * gain_f[None, :]).astype(jnp.bfloat16)
    normed_all = lax.all_gather(normed, "col", axis=0, tiled=True)
    weight_in = jnp.concatenate([proj_zx[:, 0, :], proj_zx[:, 1, :], proj_bc, proj_dt], axis=1)
    row_piece = normed_all
    mixer_in = lax.psum_scatter(
        jnp.dot(row_piece, weight_in, preferred_element_type=jnp.float32),
        "row",
        scatter_dimension=0,
        tiled=True,
    )

    def local_piece(
        mixer_value, kernel_a, offset_a, kernel_b, offset_b, decay_value, bias_value, skip_value
    ):
        return mixer_local(
            mixer_value,
            kernel_a,
            offset_a,
            kernel_b,
            offset_b,
            decay_value,
            bias_value,
            skip_value,
            seq_ids,
            live_rows,
            SCAN_BLOCK,
        )

    gated_rows, pull_back = jax.vjp(
        local_piece,
        mixer_in,
        inner_kernel,
        inner_offset,
        shared_kernel,
        shared_offset,
        decay_log,
        step_bias,
        skip_gain,
    )
    square_sum = lax.psum(jnp.sum(gated_rows * gated_rows, axis=1), "col")
    rnorm = lax.rsqrt(square_sum / DI + EPSILON)[:, None]
    out_gain = output_gain.astype(jnp.float32)
    branch = (gated_rows * rnorm * out_gain[None, :]).astype(jnp.bfloat16)
    branch_all = lax.all_gather(branch, "row", axis=0, tiled=True)
    row_piece = branch_all
    branch_out = lax.psum_scatter(
        jnp.dot(row_piece, proj_out, preferred_element_type=jnp.float32),
        "col",
        scatter_dimension=0,
        tiled=True,
    )
    block_output = (own_cols + branch_out).astype(jnp.bfloat16)
    cot_all = lax.all_gather(cotangent, "col", axis=0, tiled=True)
    row_piece = cot_all
    branch_grad = lax.psum_scatter(
        lax.dot_general(
            row_piece, proj_out, (((1,), (1,)), ((), ())), preferred_element_type=jnp.float32
        ),
        "row",
        scatter_dimension=0,
        tiled=True,
    )
    outproj_part = lax.dot_general(
        branch_all, cot_all, (((0,), (0,)), ((), ())), preferred_element_type=jnp.float32
    )
    outproj_total = outproj_part
    scaled_grad = branch_grad * out_gain[None, :]
    cross_sum = lax.psum(jnp.sum(scaled_grad * gated_rows, axis=1), "col")
    gated_grad = rnorm * scaled_grad - gated_rows * rnorm**3 * (cross_sum / DI)[:, None]
    ogain_part = jnp.sum(branch_grad * gated_rows * rnorm, axis=0)
    local_grads = pull_back(gated_grad)
    mixer_grad = local_grads[0].astype(jnp.bfloat16)
    mixer_all = lax.all_gather(mixer_grad, "row", axis=0, tiled=True)
    row_piece = mixer_all
    normed_grad = lax.psum_scatter(
        lax.dot_general(
            row_piece, weight_in, (((1,), (1,)), ((), ())), preferred_element_type=jnp.float32
        ),
        "col",
        scatter_dimension=0,
        tiled=True,
    )
    weight_grad = lax.dot_general(
        normed_all, mixer_all, (((0,), (0,)), ((), ())), preferred_element_type=jnp.float32
    )
    inproj_part = jnp.stack(
        [weight_grad[:, :inner_size], weight_grad[:, inner_size : 2 * inner_size]], axis=1
    )
    shared_part = weight_grad[:, 2 * inner_size : 2 * inner_size + 2 * state_size]
    steps_part = weight_grad[:, 2 * inner_size + 2 * state_size :]
    scaled_in = normed_grad * gain_f[None, :]
    norm_part = jnp.sum(normed_grad * normalized, axis=0)
    row_stat = lax.psum(jnp.sum(scaled_in * normalized, axis=1), "row")
    input_grad = cotangent.astype(jnp.float32) + rscale * (
        scaled_in - normalized * (row_stat / D)[:, None]
    )
    inproj_total, steps_total, outproj_total = lax.psum(
        (inproj_part, steps_part, outproj_total), "dp"
    )
    row_hot = (jnp.arange(row_count) == row_index).astype(jnp.float32)
    col_hot = (jnp.arange(col_count) == col_index).astype(jnp.float32)
    gain_slot = row_hot[:, None] * norm_part[None, :]
    shared_slot = row_hot[:, None, None] * shared_part[None, :, :]
    head_stack = jnp.stack([local_grads[5], local_grads[6], local_grads[7]], axis=0)
    head_slot = col_hot[None, :, None] * head_stack[:, None, :]
    chan_stack = jnp.concatenate(
        [local_grads[1], local_grads[2][None, :], ogain_part[None, :]], axis=0
    )
    chan_slot = col_hot[None, :, None] * chan_stack[:, None, :]
    shared_stack = jnp.concatenate([local_grads[3], local_grads[4][None, :]], axis=0)
    summed = lax.psum(
        (gain_slot, shared_slot, head_slot, chan_slot, shared_stack), ("dp", "row", "col")
    )
    gain_total = lax.dynamic_index_in_dim(summed[0], row_index, 0, keepdims=False)
    shared_total = lax.dynamic_index_in_dim(summed[1], row_index, 0, keepdims=False)
    head_total = lax.dynamic_index_in_dim(summed[2], col_index, 1, keepdims=False)
    chan_total = lax.dynamic_index_in_dim(summed[3], col_index, 1, keepdims=False)
    stack_total = summed[4]
    return (
        block_output,
        input_grad,
        gain_total,
        inproj_total,
        shared_total,
        steps_total,
        outproj_total,
        chan_total[:tap_count],
        chan_total[tap_count],
        stack_total[:tap_count],
        stack_total[tap_count],
        head_total[0],
        head_total[1],
        head_total[2],
        chan_total[tap_count + 1],
    )


def solution(mesh):
    return jax.shard_map(
        per_device,
        mesh=mesh,
        in_specs=(
            P(("dp", "col"), None),
            P(("dp", "col"), "row"),
            P(),
            P(),
            P("row"),
            P("row", None, "col"),
            P("row", None),
            P("row", "col"),
            P("col", "row"),
            P(None, "col"),
            P("col"),
            P(),
            P(),
            P("col"),
            P("col"),
            P("col"),
            P("col"),
        ),
        out_specs=(
            P(("dp", "col"), "row"),
            P(("dp", "col"), "row"),
            P("row"),
            P("row", None, "col"),
            P("row", None),
            P("row", "col"),
            P("col", "row"),
            P(None, "col"),
            P("col"),
            P(),
            P(),
            P("col"),
            P("col"),
            P("col"),
            P("col"),
        ),
        check_vma=False,
    )
```

profile of v0, /device:TPU:0, one launch (start us, length us, event | category | flops | bytes accessed | tf_op | source)
XLA Modules:
  0.0 1751.1 jit_solution(5665702625245222019)
XLA Ops:
  9.6 2.1 fusion.53
  12.8 26.0 %fusion.116 = (bf16[1280,1,2560]{2,1,0:T(2,128)(2,1)S(1)}, bf16[1280,1,2560]{2,1,0:T(2,128)(2,1)}) fusion(bf16[1280,2,2560]{2,1,0:T(2,128)(2,1)} %param.22), kind=kLoop, calls=%fused_computation.231 | loop fusion | bytes 26214400 | tf_op jit(solution)/shard_map/slice | solution.py:172
  38.8 13.5 copy_bitcast_fusion
  52.3 18.4 %fusion.41 = f32[512,5416]{1,0:T(8,128)} fusion(bf16[512,1280]{1,0:T(8,128)(2,1)} %all-gather.5.cloned.1.call-done, bf16[1280,40]{1,0:T(8,128)(2,1)S(1)} %copy.146, bf16[1280,256]{1,0:T(8,128)(2,1)S(1)} %copy-done.88, bf16[1280,2560]{1,0:T(8,128)(2,1)} %get-tuple-element.342, bf16[1280,2560]{1,0:T(8,128)(2,1)} %get-tuple-element.343), kind=kOutput, calls=%fused_computation.76 | convolution fusion | flops 7154319360 | bytes 26267648 | tf_op jit(solution)/shard_map/dot_general | solution.py:175
  71.0 9.5 fusion.121
  84.6 9.0 reduce-scatter.5.cloned.1.call-done
  96.1 2.1 slice.225
  98.2 2.9 slice.224
  102.6 4.3 fusion.39
  106.9 2.5 copy.149
  113.7 1.9 fusion.76
  116.1 11.7 fusion.5
  127.8 4.3 fusion.33
  132.1 2.1 copy.153
  134.2 4.0 multiply_reduce_fusion.10
  138.2 4.9 psum.77
  144.2 3.9 multiply_reduce_fusion.3
  148.1 4.9 psum.78
  153.0 5.8 fusion.65
  158.8 3.4 copy.154
  167.2 2.3 multiply_reduce_fusion.8
  170.0 7.2 multiply_reduce_fusion.2
  177.2 15.9 fusion.12
  195.2 2.7 reduce-window.44
  198.8 6.1 fusion.69
  205.0 11.7 bitcast_add_fusion
  216.7 3.3 copy.172
  220.1 6.9 multiply_reduce_fusion.7
  227.0 4.0 multiply_reduce_fusion.6
  231.1 6.1 fusion.66
  257.2 15.5 all-gather.11.cloned.1.call-done
  272.7 17.6 %fusion.122 = f32[1280,5416]{0,1:T(8,128)} fusion(bf16[512,1280]{1,0:T(8,128)(2,1)S(1)} %copy-done.87, bf16[512,5416]{1,0:T(8,128)(2,1)} %all-gather.11.cloned.1.call-done), kind=kOutput, calls=%fused_computation.237 | convolution fusion | flops 7098859520 | bytes 34586624 | tf_op jit(solution)/shard_map/dot_general | solution.py:252
  292.0 1.7 broadcast_multiply_fusion
  293.9 15.0 fusion.40
  309.0 8.9 fusion.120
  319.6 8.0 fusion.123
  329.2 14.7 slice_bitcast_fusion.1
  343.9 14.5 pad_maximum_fusion
  359.3 72.7 %all-reduce.36.cloned.1.call-done = (f32[2,1280,256]{2,1,0:T(8,128)}, f32[6,2,2560]{2,0,1:T(8,128)}) async-done(((f32[2,1280,256]{2,1,0:T(8,128)}, f32[6,2,2560]{2,0,1:T(8,128)}), (f32[2,1280,256]{2,1,0:T(8,128)}, f32[6,2,2560]{2,0,1:T(8,128)})) %all-reduce.36.cloned.1.call-update) | async-done | bytes 2744336 | tf_op jit(solution)/shard_map/psum | solution.py:280
  433.6 2.5 dynamic-slice_bitcast_fusion
  437.5 34.1 %reduce-scatter.11.cloned.1.call-done = f32[256,1280]{1,0:T(8,128)} async-done(((f32[512,1280]{1,0:T(8,128)}), f32[256,1280]{1,0:T(8,128)}) %reduce-scatter.11.cloned.1.call-update) | async-done | bytes 1310736 | tf_op jit(solution)/shard_map/reduce_scatter | solution.py:244
  471.7 1.9 fusion.58
  473.6 40.0 %all-reduce.30 = (f32[2,1280]{1,0:T(2,128)S(1)}, f32[5,256]{1,0:T(8,128)S(1)}, f32[3,2,40]{2,1,0:T(2,128)S(1)}) all-reduce(f32[2,1280]{1,0:T(2,128)S(1)} %broadcast_multiply_fusion.9, f32[5,256]{1,0:T(8,128)S(1)} %pad_maximum_fusion.5, ...), channel_id=1, replica_groups=mesh['dp'=8,'row'=2,'col'=2] {'dp','row','col'}, use_global_device_ids=true, to_apply=%region_28.29 | all-reduce | flops 4080 | bytes 32640 | tf_op jit(solution)/shard_map/psum | solution.py:280
  515.5 2.4 psum.79
  518.4 3.1 fusion.57
  521.5 1172.5 %all-reduce.38.cloned.1.call-done = (f32[1280,2,2560]{0,2,1:T(8,128)}, f32[1280,40]{0,1:T(8,128)}, f32[2560,1280]{1,0:T(8,128)}) async-done(((f32[1280,2,2560]{0,2,1:T(8,128)}, f32[1280,40]{0,1:T(8,128)}, f32[2560,1280]{1,0:T(8,128)}), (f32[1280,2,2560]{0,2,1:T(8,128)}, f32[1280,40]{0,1:T(8,128)}, f32[2560,1280]{1,0:T(8,128)})) %all-reduce.38.cloned.1.call-update) | async-done | bytes 39526416 | tf_op jit(solution)/shard_map/psum | solution.py:266
  1694.1 38.8 %copy.176 = f32[1280,2,2560]{2,1,0:T(2,128)} copy(f32[1280,2,2560]{0,2,1:T(8,128)} %get-tuple-element.270) | data formatting | bytes 52428800
  1733.5 10.5 copy.205
  (332 shorter events, 56.2 us)
Async XLA Ops:
  7.2 45.1 %all-gather.5.cloned.1.call-start = ((), (), s32[]{:S(2)}) async-start(), calls=%async_computation.4 | async-start | bytes 1966080 | tf_op jit(solution)/shard_map/all_gather | solution.py:171
  11.8 59.2 %all-gather.9.cloned.1.call-start = ((), (), s32[]{:S(2)}) async-start(), calls=%async_computation.8 | async-start | bytes 1966080 | tf_op jit(solution)/shard_map/all_gather | solution.py:222
  12.6 81.0 %reduce-scatter.5.cloned.1.call-start = ((), (), s32[]{:S(2)}) async-start(), calls=%async_computation.5 | async-start | bytes 16908288 | tf_op jit(solution)/shard_map/reduce_scatter | solution.py:174
  12.8 39.5 %copy-start.29 = (bf16[1280,40]{1,0:T(8,128)(2,1)}, bf16[1280,40]{1,0:T(8,128)(2,1)S(1)}, u32[]{:S(2)}) copy-start(bf16[1280,40]{1,0:T(8,128)(2,1)S(1)} %copy.146) | copy-start | bytes 307204
  38.8 13.5 copy-start.88
  70.8 73.4 %reduce-scatter.9.cloned.1.call-start = ((), (), s32[]{:S(2)}) async-start(), calls=%async_computation.9 | async-start | bytes 7864320 | tf_op jit(solution)/shard_map/reduce_scatter | solution.py:224
  80.6 13.0 copy-start.77
  80.6 192.1 %all-gather.11.cloned.1.call-start = ((), (), s32[]{:S(2)}) async-start(), calls=%async_computation.10 | async-start | bytes 8454144 | tf_op jit(solution)/shard_map/all_gather | solution.py:242
  82.5 19.0 %copy-start.37 = (f32[2560]{0:T(1024)}, f32[2560]{0:T(1024)S(1)}, u32[]{:S(2)}) copy-start(f32[2560]{0:T(1024)S(1)} %get-tuple-element.261) | copy-start | bytes 30724
  82.5 19.0 %copy-start.39 = (f32[2560]{0:T(1024)}, f32[2560]{0:T(1024)S(1)}, u32[]{:S(2)}) copy-start(f32[2560]{0:T(1024)S(1)} %get-tuple-element.263) | copy-start | bytes 30724
  82.5 19.0 %copy-start.41 = (f32[2560]{0:T(1024)}, f32[2560]{0:T(1024)S(1)}, u32[]{:S(2)}) copy-start(f32[2560]{0:T(1024)S(1)} %get-tuple-element.262) | copy-start | bytes 30724
  82.5 19.0 %copy-start.43 = (f32[2560]{0:T(1024)}, f32[2560]{0:T(1024)S(1)}, u32[]{:S(2)}) copy-start(f32[2560]{0:T(1024)S(1)} %get-tuple-element.264) | copy-start | bytes 30724
  82.5 12.0 copy-start.79
  82.6 15.6 copy-start.71
  82.6 45.1 %copy-start.52 = (f32[256]{0:T(256)}, f32[256]{0:T(256)S(1)}, u32[]{:S(2)}) copy-start(f32[256]{0:T(256)S(1)} %get-tuple-element.124) | copy-start | bytes 3076
  83.2 18.3 %copy-start.56 = (f32[256]{0:T(256)}, f32[256]{0:T(256)S(1)}, u32[]{:S(2)}) copy-start(f32[256]{0:T(256)S(1)} %get-tuple-element.335) | copy-start | bytes 3076
  83.2 18.3 %copy-start.59 = (f32[256]{0:T(256)}, f32[256]{0:T(256)S(1)}, u32[]{:S(2)}) copy-start(f32[256]{0:T(256)S(1)} %get-tuple-element.336) | copy-start | bytes 3076
  83.2 30.5 %copy-start.54 = (f32[256]{0:T(256)}, f32[256]{0:T(256)S(1)}, u32[]{:S(2)}) copy-start(f32[256]{0:T(256)S(1)} %get-tuple-element.334) | copy-start | bytes 3076
  95.4 17.4 copy-start.66
  109.4 18.4 %copy-start = (f32[256,2560]{0,1:T(8,128)}, f32[256,2560]{0,1:T(8,128)S(1)}, u32[]{:S(2)}) copy-start(f32[256,2560]{0,1:T(8,128)S(1)} %copy.149) | copy-start | bytes 7864324
  112.8 14.9 copy-start.19
  115.6 12.1 copy-start.23
  116.0 11.7 copy-start.83
  165.1 72.1 %copy-start.24 = (pred[256,256]{1,0:T(8,128)(4,1)}, pred[256,256]{1,0:T(8,128)(4,1)S(1)}, u32[]{:S(2)}) copy-start(pred[256,256]{1,0:T(8,128)(4,1)S(1)} %and_and_fusion) | copy-start | bytes 196612
  165.1 29.8 %copy-start.61 = (f32[1,256]{1,0:T(1,128)}, f32[1,256]{1,0:T(1,128)S(1)}, u32[]{:S(2)}) copy-start(f32[1,256]{1,0:T(1,128)S(1)} %slice_convert_fusion) | copy-start | bytes 3076
  169.9 7.3 copy-start.31
  193.1 44.2 %copy-start.26 = (f32[256,256]{1,0:T(8,128)}, f32[256,256]{1,0:T(8,128)S(1)}, u32[]{:S(2)}) copy-start(f32[256,256]{1,0:T(8,128)S(1)} %get-tuple-element.248) | copy-start | bytes 786436
  194.8 10.1 copy-start.68
  195.1 9.8 copy-start.32
  195.1 9.8 copy-start.84
  231.1 8.3 copy-start.22
  231.1 8.3 copy-start.25
  231.1 9.7 copy-start.20
  231.1 9.7 copy-start.58
  237.8 9.2 copy-start.15
  240.8 7.5 copy-start.42
  255.4 17.2 copy-start.87
  255.5 53.5 %all-gather.7.cloned.1.call-start = ((), (), s32[]{:S(2)}) async-start(), calls=%async_computation.6 | async-start | bytes 3932160 | tf_op jit(solution)/shard_map/all_gather | solution.py:213
  256.3 175.7 %all-reduce.36.cloned.1.call-start = ((), (), s32[]{:S(2)}) async-start(), calls=%async_computation.12 | async-start | bytes 5570560 | tf_op jit(solution)/shard_map/psum | solution.py:280
  293.8 177.8 %reduce-scatter.11.cloned.1.call-start = ((), (), s32[]{:S(2)}) async-start(), calls=%async_computation.11 | async-start | bytes 3932160 | tf_op jit(solution)/shard_map/reduce_scatter | solution.py:244
  308.9 209.5 %reduce-scatter.7.cloned.1.call-start = ((), (), s32[]{:S(2)}) async-start(), calls=%async_computation.7 | async-start | bytes 3932160 | tf_op jit(solution)/shard_map/reduce_scatter | solution.py:215
  317.9 1376.2 %all-reduce.38.cloned.1.call-start = ((), (), s32[]{:S(2)}) async-start(), calls=%async_computation.13 | async-start | bytes 79052800 | tf_op jit(solution)/shard_map/psum | solution.py:266
  358.5 113.2 %copy-start.16 = (bf16[256,2560]{1,0:T(8,128)(2,1)S(1)}, bf16[256,2560]{1,0:T(8,128)(2,1)}, u32[]{:S(2)}) copy-start(bf16[256,2560]{1,0:T(8,128)(2,1)} %param.17) | copy-start | bytes 3932164
  358.5 113.2 %copy-start.36 = (f32[1280]{0:T(1024)S(1)}, f32[1280]{0:T(1024)}, u32[]{:S(2)}) copy-start(f32[1280]{0:T(1024)} %copy-done.35) | copy-start | bytes 15364
  358.5 113.2 %copy-start.64 = (f32[256]{0:T(256)S(1)}, f32[256]{0:T(256)}, u32[]{:S(2)}) copy-start(f32[256]{0:T(256)} %copy-done.63) | copy-start | bytes 3076
  358.5 159.9 %copy-start.18 = (bf16[256,1280]{1,0:T(8,128)(2,1)S(1)}, bf16[256,1280]{1,0:T(8,128)(2,1)}, u32[]{:S(2)}) copy-start(bf16[256,1280]{1,0:T(8,128)(2,1)} %param.18) | copy-start | bytes 1966084
  471.7 46.8 %copy-start.17 = (f32[256,1280]{1,0:T(8,128)S(1)}, f32[256,1280]{1,0:T(8,128)}, u32[]{:S(2)}) copy-start(f32[256,1280]{1,0:T(8,128)} %reduce-scatter.11.cloned.1.call-done) | copy-start | bytes 3932164
  1694.0 38.8 %copy-start.34 = (f32[1280,40]{0,1:T(8,128)S(1)}, f32[1280,40]{0,1:T(8,128)}, u32[]{:S(2)}) copy-start(f32[1280,40]{0,1:T(8,128)} %get-tuple-element.349) | copy-start | bytes 614404
  (59 other events, 172.4 us)
Sparse Core Ops, SparseCore 0:
  11.9 26.9 all-gather.4
  40.4 24.2 all-gather.8
  70.9 22.6 reduce-scatter.4
  95.7 14.4 reduce-scatter.8
  255.6 17.0 all-gather.10
  274.7 12.5 all-gather.6
  294.3 137.5 all-reduce.35
  434.3 37.3 reduce-scatter.10
  473.9 38.2 reduce-scatter.6
  518.2 1175.8 all-reduce.37
where the time goes:
time: 1760 us; the launch traced here: 1750 us
  waiting for transfers between devices  1300 us (74%)
  local copies, waits for them, and re-layouts  152 us (9%)
  matrix products  146 us (8%)
  other arithmetic  78.7 us (4%)
  blocking collectives  52.3 us (3%)
    psum x1, waiting for transfers between devices, per_device(): lax.psum((inproj_part, steps_part, outproj_total), 'dp')  1170 us
    psum x1, waiting for transfers between devices, per_device(): lax.psum((gain_slot, shared_slot, head_slot, chan_slot, shared_stack), ('...  72.7 us
    unnamed x196, local copies, waits for them, and re-layouts  59.1 us
    psum x1, blocking collectives, per_device(): lax.psum((gain_slot, shared_slot, head_slot, chan_slot, shared_stack), ('...  40 us
    dot_general x3, matrix products, one_block(): within = jnp.einsum('tsh,shp->thp', weights, vals, precision=PRECISE)  39.3 us
  transfers between devices with their start and end apart: 10, of which 5 were waited for; matrix products, arithmetic and copies ran while one was open for 12% of the time, Pallas kernels for 0%

commit v1 on v0

--- a/solution.py
+++ b/solution.py
@@ -277,9 +277,9 @@
     )
     chan_slot = col_hot[None, :, None] * chan_stack[:, None, :]
     shared_stack = jnp.concatenate([local_grads[3], local_grads[4][None, :]], axis=0)
-    summed = lax.psum(
-        (gain_slot, shared_slot, head_slot, chan_slot, shared_stack), ("dp", "row", "col")
-    )
+    summed = (gain_slot, shared_slot, head_slot, chan_slot, shared_stack)
+    for mesh_axis in (("row", "col"), "dp"):
+        summed = lax.psum(summed, mesh_axis)
     gain_total = lax.dynamic_index_in_dim(summed[0], row_index, 0, keepdims=False)
     shared_total = lax.dynamic_index_in_dim(summed[1], row_index, 0, keepdims=False)
     head_total = lax.dynamic_index_in_dim(summed[2], col_index, 1, keepdims=False)

time: 1760 us -> 1780 us (1.011)
    psum x1, waiting for transfers between devices: 1170 us -> 1250 us  [per_device(): lax.psum((inproj_part, steps_part, outproj_total), 'dp')]
    psum x1, waiting for transfers between devices: 72.7 us -> 0.01 us  [per_device(): summed = lax.psum(summed, mesh_axis)]
    psum x1 -> x2, blocking collectives: 40 us -> 49.1 us  [per_device(): summed = lax.psum(summed, mesh_axis)]
    unnamed x196 -> x198, local copies, waits for them, and re-layouts: 59.1 us -> 59.2 us
  transfers between devices with their start and end apart: 10 -> 10, of which waited for: 5 -> 4; matrix products, arithmetic and copies ran while one was open for 12% -> 12% of each run, Pallas kernels for 0% -> 0%
where the time goes in v1:
time: 1780 us; the launch traced here: 1770 us
  waiting for transfers between devices  1310 us (74%)
  local copies, waits for them, and re-layouts  151 us (8%)
  matrix products  145 us (8%)
  other arithmetic  78.7 us (4%)
  blocking collectives  61.4 us (3%)
    psum x1, waiting for transfers between devices, per_device(): lax.psum((inproj_part, steps_part, outproj_total), 'dp')  1250 us
    unnamed x198, local copies, waits for them, and re-layouts  59.2 us
    psum x2, blocking collectives, per_device(): summed = lax.psum(summed, mesh_axis)  49.1 us
    dot_general x3, matrix products, one_block(): within = jnp.einsum('tsh,shp->thp', weights, vals, precision=PRECISE)  39.3 us
    reduce_scatter x1, waiting for transfers between devices, per_device(): lax.psum_scatter(lax.dot_general(row_piece, weight_in, (((1,), (1,)), (()...  38.2 us
  transfers between devices with their start and end apart: 10, of which 4 were waited for; matrix products, arithmetic and copies ran while one was open for 12% of the time, Pallas kernels for 0%

profile of v1, /device:TPU:0, one launch (start us, length us, event | category | flops | bytes accessed | tf_op | source)
XLA Modules:
  0.0 1768.5 jit_solution(12388100788643615600)
XLA Ops:
  9.6 2.1 fusion.53
  12.8 26.0 %fusion.116 = (bf16[1280,1,2560]{2,1,0:T(2,128)(2,1)S(1)}, bf16[1280,1,2560]{2,1,0:T(2,128)(2,1)}) fusion(bf16[1280,2,2560]{2,1,0:T(2,128)(2,1)} %param.22), kind=kLoop, calls=%fused_computation.231 | loop fusion | bytes 26214400 | tf_op jit(solution)/shard_map/slice | solution.py:172
  38.8 13.5 copy_bitcast_fusion
  52.3 18.4 %fusion.41 = f32[512,5416]{1,0:T(8,128)} fusion(bf16[512,1280]{1,0:T(8,128)(2,1)} %all-gather.5.cloned.1.call-done, bf16[1280,40]{1,0:T(8,128)(2,1)S(1)} %copy.146, bf16[1280,256]{1,0:T(8,128)(2,1)S(1)} %copy-done.89, bf16[1280,2560]{1,0:T(8,128)(2,1)} %get-tuple-element.347, bf16[1280,2560]{1,0:T(8,128)(2,1)} %get-tuple-element.348), kind=kOutput, calls=%fused_computation.76 | convolution fusion | flops 7154319360 | bytes 26267648 | tf_op jit(solution)/shard_map/dot_general | solution.py:175
  71.0 9.5 fusion.121
  84.6 9.0 reduce-scatter.5.cloned.1.call-done
  96.1 2.1 slice.225
  98.2 2.9 slice.224
  102.6 4.3 fusion.39
  106.9 2.5 copy.149
  113.7 1.9 fusion.76
  116.1 11.7 fusion.5
  127.8 4.3 fusion.33
  132.1 2.1 copy.153
  134.2 4.0 multiply_reduce_fusion.10
  138.2 4.9 psum.112
  144.2 3.9 multiply_reduce_fusion.3
  148.1 4.9 psum.113
  153.0 5.8 fusion.65
  158.8 3.4 copy.154
  167.2 2.3 multiply_reduce_fusion.8
  170.0 7.2 multiply_reduce_fusion.2
  177.2 15.9 fusion.12
  195.2 2.7 reduce-window.44
  198.8 6.1 fusion.69
  205.0 11.7 bitcast_add_fusion
  216.7 3.3 copy.172
  220.1 6.9 multiply_reduce_fusion.7
  227.0 4.0 multiply_reduce_fusion.6
  231.1 6.1 fusion.66
  253.7 1.7 add_convert_fusion
  257.2 15.5 all-gather.11.cloned.1.call-done
  272.7 17.6 fusion.122
  292.0 1.7 broadcast_multiply_fusion
  293.9 15.0 fusion.40
  309.0 8.8 fusion.120
  319.5 8.0 fusion.123
  329.1 15.2 slice_bitcast_fusion.1
  344.3 14.5 pad_maximum_fusion
  359.6 38.2 %reduce-scatter.11.cloned.1.call-done = f32[256,1280]{1,0:T(8,128)} async-done(((f32[512,1280]{1,0:T(8,128)}), f32[256,1280]{1,0:T(8,128)}) %reduce-scatter.11.cloned.1.call-update) | async-done | bytes 1310736 | tf_op jit(solution)/shard_map/reduce_scatter | solution.py:244
  397.8 1.9 fusion.58
  399.8 12.0 all-reduce.32
  411.8 37.1 %all-reduce.30 = (f32[2,1280]{1,0:T(2,128)S(1)}, f32[5,256]{1,0:T(8,128)S(1)}, f32[3,2,40]{2,1,0:T(2,128)S(1)}) all-reduce(f32[2,1280]{1,0:T(2,128)S(1)} %get-tuple-element.273, f32[5,256]{1,0:T(8,128)S(1)} %get-tuple-element.274, f32[3,2,40]{2,1,0:T(2,128)S(1)} %get-tuple-element.275), channel_id=1, replica_groups=mesh['dp'=8,'row'=2,'col'=2] {'dp'}, use_global_device_ids=true, to_apply=%region_29.30 | all-reduce | flops 4080 | bytes 32640 | tf_op jit(solution)/shard_map/psum | solution.py:282
  450.7 2.4 psum.114
  453.7 3.1 fusion.57
  456.7 1250.3 %all-reduce.37.cloned.1.call-done = (f32[1280,2,2560]{0,2,1:T(8,128)}, f32[2,1280,256]{2,1,0:T(8,128)}, f32[1280,40]{0,1:T(8,128)}, f32[2560,1280]{1,0:T(8,128)}, f32[6,2,2560]{2,0,1:T(8,128)}) async-done(((f32[1280,2,2560]{0,2,1:T(8,128)}, f32[2,1280,256]{2,1,0:T(8,128)}, f32[1280,40]{0,1:T(8,128)}, f32[2560,1280]{1,0:T(8,128)}, f32[6,2,2560]{2,0,1:T(8,128)}), (f32[1280,2,2560]{0,2,1:T(8,128)}, ...) | async-done | bytes 42270736 | tf_op jit(solution)/shard_map/psum | solution.py:266
  1707.1 38.9 %copy.176 = f32[1280,2,2560]{2,1,0:T(2,128)} copy(f32[1280,2,2560]{0,2,1:T(8,128)} %get-tuple-element.268) | data formatting | bytes 52428800
  1751.0 10.5 copy.207
  (335 shorter events, 55.7 us)
Async XLA Ops:
  7.2 45.1 %all-gather.5.cloned.1.call-start = ((), (), s32[]{:S(2)}) async-start(), calls=%async_computation.4 | async-start | bytes 1966080 | tf_op jit(solution)/shard_map/all_gather | solution.py:171
  11.8 59.2 %all-gather.9.cloned.1.call-start = ((), (), s32[]{:S(2)}) async-start(), calls=%async_computation.8 | async-start | bytes 1966080 | tf_op jit(solution)/shard_map/all_gather | solution.py:222
  12.6 81.0 %reduce-scatter.5.cloned.1.call-start = ((), (), s32[]{:S(2)}) async-start(), calls=%async_computation.5 | async-start | bytes 16908288 | tf_op jit(solution)/shard_map/reduce_scatter | solution.py:174
  12.8 39.5 %copy-start.30 = (bf16[1280,40]{1,0:T(8,128)(2,1)}, bf16[1280,40]{1,0:T(8,128)(2,1)S(1)}, u32[]{:S(2)}) copy-start(bf16[1280,40]{1,0:T(8,128)(2,1)S(1)} %copy.146) | copy-start | bytes 307204
  38.8 13.5 copy-start.89
  70.8 73.4 %reduce-scatter.9.cloned.1.call-start = ((), (), s32[]{:S(2)}) async-start(), calls=%async_computation.9 | async-start | bytes 7864320 | tf_op jit(solution)/shard_map/reduce_scatter | solution.py:224
  80.6 13.0 copy-start.78
  80.6 192.1 %all-gather.11.cloned.1.call-start = ((), (), s32[]{:S(2)}) async-start(), calls=%async_computation.10 | async-start | bytes 8454144 | tf_op jit(solution)/shard_map/all_gather | solution.py:242
  82.5 19.0 %copy-start.38 = (f32[2560]{0:T(1024)}, f32[2560]{0:T(1024)S(1)}, u32[]{:S(2)}) copy-start(f32[2560]{0:T(1024)S(1)} %get-tuple-element.261) | copy-start | bytes 30724
  82.5 19.0 %copy-start.40 = (f32[2560]{0:T(1024)}, f32[2560]{0:T(1024)S(1)}, u32[]{:S(2)}) copy-start(f32[2560]{0:T(1024)S(1)} %get-tuple-element.263) | copy-start | bytes 30724
  82.5 19.0 %copy-start.42 = (f32[2560]{0:T(1024)}, f32[2560]{0:T(1024)S(1)}, u32[]{:S(2)}) copy-start(f32[2560]{0:T(1024)S(1)} %get-tuple-element.262) | copy-start | bytes 30724
  82.5 19.0 %copy-start.44 = (f32[2560]{0:T(1024)}, f32[2560]{0:T(1024)S(1)}, u32[]{:S(2)}) copy-start(f32[2560]{0:T(1024)S(1)} %get-tuple-element.264) | copy-start | bytes 30724
  82.5 12.0 copy-start.80
  82.6 15.6 copy-start.72
  82.6 45.1 %copy-start.53 = (f32[256]{0:T(256)}, f32[256]{0:T(256)S(1)}, u32[]{:S(2)}) copy-start(f32[256]{0:T(256)S(1)} %get-tuple-element.124) | copy-start | bytes 3076
  83.2 18.3 %copy-start.57 = (f32[256]{0:T(256)}, f32[256]{0:T(256)S(1)}, u32[]{:S(2)}) copy-start(f32[256]{0:T(256)S(1)} %get-tuple-element.340) | copy-start | bytes 3076
  83.2 18.3 %copy-start.60 = (f32[256]{0:T(256)}, f32[256]{0:T(256)S(1)}, u32[]{:S(2)}) copy-start(f32[256]{0:T(256)S(1)} %get-tuple-element.341) | copy-start | bytes 3076
  83.2 30.5 %copy-start.55 = (f32[256]{0:T(256)}, f32[256]{0:T(256)S(1)}, u32[]{:S(2)}) copy-start(f32[256]{0:T(256)S(1)} %get-tuple-element.339) | copy-start | bytes 3076
  95.4 17.4 copy-start.67
  109.4 18.4 %copy-start = (f32[256,2560]{0,1:T(8,128)}, f32[256,2560]{0,1:T(8,128)S(1)}, u32[]{:S(2)}) copy-start(f32[256,2560]{0,1:T(8,128)S(1)} %copy.149) | copy-start | bytes 7864324
  112.8 14.9 copy-start.19
  115.6 12.1 copy-start.23
  116.0 11.7 copy-start.84
  165.1 72.1 %copy-start.24 = (pred[256,256]{1,0:T(8,128)(4,1)}, pred[256,256]{1,0:T(8,128)(4,1)S(1)}, u32[]{:S(2)}) copy-start(pred[256,256]{1,0:T(8,128)(4,1)S(1)} %and_and_fusion) | copy-start | bytes 196612
  165.1 29.8 %copy-start.62 = (f32[1,256]{1,0:T(1,128)}, f32[1,256]{1,0:T(1,128)S(1)}, u32[]{:S(2)}) copy-start(f32[1,256]{1,0:T(1,128)S(1)} %slice_convert_fusion) | copy-start | bytes 3076
  169.9 7.3 copy-start.32
  193.1 44.1 %copy-start.26 = (f32[256,256]{1,0:T(8,128)}, f32[256,256]{1,0:T(8,128)S(1)}, u32[]{:S(2)}) copy-start(f32[256,256]{1,0:T(8,128)S(1)} %get-tuple-element.248) | copy-start | bytes 786436
  194.8 10.1 copy-start.69
  195.1 9.8 copy-start.33
  195.1 9.8 copy-start.85
  231.1 8.3 copy-start.22
  231.1 8.3 copy-start.25
  231.1 9.7 copy-start.20
  231.1 9.7 copy-start.59
  237.8 9.2 copy-start.15
  240.8 7.5 copy-start.43
  255.4 17.2 copy-start.88
  255.5 53.5 %all-gather.7.cloned.1.call-start = ((), (), s32[]{:S(2)}) async-start(), calls=%async_computation.6 | async-start | bytes 3932160 | tf_op jit(solution)/shard_map/all_gather | solution.py:213
  256.3 102.5 %all-reduce.39.cloned.1.call-start = ((), (), s32[]{:S(2)}) async-start(), calls=%async_computation.13 | async-start | bytes 5570560 | tf_op jit(solution)/shard_map/psum | solution.py:282
  293.8 104.0 %reduce-scatter.11.cloned.1.call-start = ((), (), s32[]{:S(2)}) async-start(), calls=%async_computation.11 | async-start | bytes 3932160 | tf_op jit(solution)/shard_map/reduce_scatter | solution.py:244
  308.9 144.8 %reduce-scatter.7.cloned.1.call-start = ((), (), s32[]{:S(2)}) async-start(), calls=%async_computation.7 | async-start | bytes 3932160 | tf_op jit(solution)/shard_map/reduce_scatter | solution.py:215
  317.8 1389.3 %all-reduce.37.cloned.1.call-start = ((), (), s32[]{:S(2)}) async-start(), calls=%async_computation.12 | async-start | bytes 84623360 | tf_op jit(solution)/shard_map/psum | solution.py:266
  358.8 39.0 %copy-start.16 = (bf16[256,2560]{1,0:T(8,128)(2,1)S(1)}, bf16[256,2560]{1,0:T(8,128)(2,1)}, u32[]{:S(2)}) copy-start(bf16[256,2560]{1,0:T(8,128)(2,1)} %param.17) | copy-start | bytes 3932164
  358.8 39.0 %copy-start.37 = (f32[1280]{0:T(1024)S(1)}, f32[1280]{0:T(1024)}, u32[]{:S(2)}) copy-start(f32[1280]{0:T(1024)} %copy-done.36) | copy-start | bytes 15364
  358.8 39.0 %copy-start.65 = (f32[256]{0:T(256)S(1)}, f32[256]{0:T(256)}, u32[]{:S(2)}) copy-start(f32[256]{0:T(256)} %copy-done.64) | copy-start | bytes 3076
  358.9 94.8 %copy-start.18 = (bf16[256,1280]{1,0:T(8,128)(2,1)S(1)}, bf16[256,1280]{1,0:T(8,128)(2,1)}, u32[]{:S(2)}) copy-start(bf16[256,1280]{1,0:T(8,128)(2,1)} %param.18) | copy-start | bytes 1966084
  397.8 55.8 %copy-start.17 = (f32[256,1280]{1,0:T(8,128)S(1)}, f32[256,1280]{1,0:T(8,128)}, u32[]{:S(2)}) copy-start(f32[256,1280]{1,0:T(8,128)} %reduce-scatter.11.cloned.1.call-done) | copy-start | bytes 3932164
  1707.1 40.5 %copy-start.27 = (f32[2,1280,256]{2,1,0:T(8,128)S(1)}, f32[2,1280,256]{2,1,0:T(8,128)}, u32[]{:S(2)}) copy-start(f32[2,1280,256]{2,1,0:T(8,128)} %get-tuple-element.269) | copy-start | bytes 7864324
  (60 other events, 176.7 us)
Sparse Core Ops, SparseCore 0:
  11.9 26.9 all-gather.4
  40.4 24.2 all-gather.8
  70.9 22.6 reduce-scatter.4
  95.7 14.4 reduce-scatter.8
  255.6 17.0 all-gather.10
  274.7 12.5 all-gather.6
  293.9 63.9 all-reduce.38
  360.1 37.6 reduce-scatter.10
  400.1 38.0 reduce-scatter.6
  443.9 1263.0 all-reduce.36
